TPU v7x, 512 devices: a whole 4x4x16 slice. The times are simulated.
512 devices in a mesh: expert: 8 (over z_lo, core), dp: 64 (over z_hi, x, y).
Axes of the slice: x: 4, y: 4, z: 16 (z_hi: 4, z_lo: 4; z = z_hi * 4 + z_lo), core: 2. Of those that a mesh axis runs over, the one named last changes fastest.
Arguments:
- x_rows: bfloat16 [8, 64, 8, 2, 3072], P('expert', 'dp'), may hold values from -6 to 6
- cot_rows: bfloat16 [8, 64, 8, 2, 3072], P('expert', 'dp'), may hold values from -3 to 3
- counts: int32 [8, 64, 8], P(None, 'dp'), may hold values from 0 to 2, as said below
- w_gate: bfloat16 [8, 3072, 8192], P('expert', None, 'dp'), may hold values from -0.109375 to 0.109375
- w_up: bfloat16 [8, 3072, 8192], P('expert', None, 'dp'), may hold values from -0.109375 to 0.109375
- w_down: bfloat16 [8, 8192, 3072], P('expert', 'dp'), may hold values from -0.0625 to 0.0625
- kept_blocks: int32 [8], P('expert'), may hold values from 16 to 64
- block_rank: int32 [8, 64], P('expert', 'dp'), may hold values from 0 to 63, each once within a row
Outputs:
- grad_rows: bfloat16 [8, 64, 8, 2, 3072], P('expert', 'dp')
- grad_gate: bfloat16 [8, 3072, 8192], P('expert', None, 'dp')
- grad_up: bfloat16 [8, 3072, 8192], P('expert', None, 'dp')
- grad_down: bfloat16 [8, 8192, 3072], P('expert', 'dp')
Inputs may be any that keep to these rules, and one draw needn't show every extreme that they name: The live slots of a source's buffer for an expert are its first ones. For every expert e and index d the sum over sources s of counts[s, d, e] is at most 4, and it equals 4 for every d of some expert.
All inputs are finite; a program needn't handle non-finite values.
Results may differ from a plain program's by a relative error of at most 0.005.
Values may be sent and summed in bfloat16 or wider, within the bound.
No kernel may reach another device: no remote copies, remote signals or barrier semaphores. Data moves between devices by JAX's collectives and lax.ppermute only.
A program may use at most 64 MiB of HBM per device.

v0:
```python
import jax
import jax.numpy as jnp
from jax import lax
from jax.sharding import PartitionSpec as P

LIVE = 4


def compact_matrix(slot_counts, live_rows, capacity):
    sources = slot_counts.shape[0]
    within_slot = jnp.tile(jnp.arange(capacity, dtype=jnp.int32), sources)
    count_slot = jnp.repeat(slot_counts, capacity)
    earlier = jnp.arange(sources)[None, :] < jnp.arange(sources)[:, None]
    offsets = jnp.repeat(jnp.sum(jnp.where(earlier, slot_counts[None, :], 0), axis=1), capacity)
    target = offsets + within_slot
    alive = within_slot < count_slot
    row_index = jnp.arange(live_rows, dtype=jnp.int32)[:, None]
    return ((row_index == target[None, :]) & alive[None, :]).astype(jnp.bfloat16)


def contract(left, right, left_dim, right_dim):
    return lax.dot_general(
        left, right, (((left_dim,), (right_dim,)), ((), ())), preferred_element_type=jnp.float32
    )


def body(x_rows, cot_rows, counts, w_gate, w_up, w_down, kept_blocks, block_rank):
    expert_count = x_rows.shape[2]
    capacity = x_rows.shape[3]
    model_width = x_rows.shape[4]
    slot_rows = x_rows.reshape(expert_count, capacity, model_width)
    slot_cots = cot_rows.reshape(expert_count, capacity, model_width)
    my_expert = lax.axis_index("expert")
    picked = jnp.arange(expert_count, dtype=jnp.int32)[None, :] == my_expert
    own_counts = jnp.sum(jnp.where(picked, counts[:, 0, :], 0), axis=1)
    chooser = compact_matrix(own_counts, LIVE, capacity)

    def pack_rows(received):
        flat_rows = received.reshape(-1, model_width)
        return jnp.dot(chooser, flat_rows, preferred_element_type=jnp.float32).astype(jnp.bfloat16)

    got_rows, got_cots = (
        lax.all_to_all(slot_rows, "expert", split_axis=0, concat_axis=0, tiled=True),
        lax.all_to_all(slot_cots, "expert", split_axis=0, concat_axis=0, tiled=True),
    )
    group_rows, group_cots = (
        lax.all_gather(pack_rows(got_rows), "dp", axis=0, tiled=True),
        lax.all_gather(pack_rows(got_cots), "dp", axis=0, tiled=True),
    )
    gate_weight = w_gate[0]
    up_weight = w_up[0]
    down_weight = w_down[0]
    keep_mask = (block_rank.reshape(()) < kept_blocks.reshape(())).astype(jnp.float32)
    gate_pre = jnp.dot(group_rows, gate_weight, preferred_element_type=jnp.float32)
    up_pre = jnp.dot(group_rows, up_weight, preferred_element_type=jnp.float32)
    sigmoid_gate = jax.nn.sigmoid(gate_pre)
    activated = gate_pre * sigmoid_gate
    hidden = (activated * up_pre * keep_mask).astype(jnp.bfloat16)
    hidden_grad = contract(group_cots, down_weight, 1, 1)
    up_grad = (hidden_grad * activated * keep_mask).astype(jnp.bfloat16)
    gate_grad = (
        hidden_grad * up_pre * sigmoid_gate * (1.0 + gate_pre * (1.0 - sigmoid_gate)) * keep_mask
    ).astype(jnp.bfloat16)
    grad_down = contract(hidden, group_cots, 0, 0).astype(jnp.bfloat16)
    grad_gate = contract(group_rows, gate_grad, 0, 0).astype(jnp.bfloat16)
    grad_up = contract(group_rows, up_grad, 0, 0).astype(jnp.bfloat16)
    whole_term = contract(gate_grad, gate_weight, 1, 1) + contract(up_grad, up_weight, 1, 1)
    row_grads = lax.psum_scatter(whole_term, "dp", scatter_dimension=0, tiled=True)
    row_grads = row_grads.astype(jnp.bfloat16)
    slot_grads = contract(chooser, row_grads, 0, 0).astype(jnp.bfloat16)
    slot_grads = slot_grads.reshape(expert_count, capacity, model_width)
    returned = lax.all_to_all(slot_grads, "expert", split_axis=0, concat_axis=0, tiled=True)
    grad_rows = returned.reshape(1, 1, expert_count, capacity, model_width)
    return (grad_rows, grad_gate[None], grad_up[None], grad_down[None])


def solution(mesh):
    in_specs = (
        P("expert", "dp", None, None, None),
        P("expert", "dp", None, None, None),
        P(None, "dp", None),
        P("expert", None, "dp"),
        P("expert", None, "dp"),
        P("expert", "dp", None),
        P("expert"),
        P("expert", "dp"),
    )
    out_specs = (
        P("expert", "dp", None, None, None),
        P("expert", None, "dp"),
        P("expert", None, "dp"),
        P("expert", "dp", None),
    )
    return jax.shard_map(body, mesh=mesh, in_specs=in_specs, out_specs=out_specs, check_vma=False)
```

profile of v0, /device:TPU:1, one launch (start us, length us, event | category | flops | bytes accessed | tf_op | source)
XLA Modules:
  0.0 771.1 jit_solution(6798377600060864773)
XLA Ops:
  7.2 10.3 %all-to-all-start.1 = ((bf16[8,2,3072]{2,1,0:T(2,128)(2,1)}), bf16[8,2,3072]{2,1,0:T(2,128)(2,1)S(1)}, u32[]{:S(2)}, u32[]{:S(2)}) async-start(bf16[8,2,3072]{2,1,0:T(2,128)(2,1)} %bitcast.47), calls=%async_computation.1 | async-start | bytes 196608 | tf_op jit(solution)/shard_map/all_to_all | solution.py:43
  17.5 0.8 select_reduce_fusion.1
  18.3 0.1 iota_compare_fusion
  18.4 0.1 lt.30
  18.4 0.1 select_reduce_fusion
  18.6 0.1 iota_add_fusion
  18.6 0.1 add.22
  18.7 4.3 all-to-all-done.1
  23.0 0.7 fusion.4
  23.8 0.0 all-gather.5.cloned.1.call-start
  23.8 9.6 %all_to_all.15 = bf16[8,2,3072]{2,1,0:T(2,128)(2,1)S(1)} all-to-all(bf16[8,2,3072]{2,1,0:T(2,128)(2,1)} %bitcast.48), channel_id=1, replica_groups=mesh['expert'=8,'dp'=64] {'expert'}, dimensions={0} | all-to-all | bytes 196608 | tf_op jit(solution)/shard_map/all_to_all | solution.py:44
  33.5 0.7 fusion.3
  35.6 1.3 dynamic-slice
  37.5 93.3 %all-gather.7.cloned.1.call-done = bf16[64,4,3072]{2,1,0:T(4,128)(2,1)} async-done(((bf16[1,4,3072]{2,1,0:T(4,128)(2,1)}), bf16[64,4,3072]{2,1,0:T(4,128)(2,1)}) %all-gather.7.cloned.1.call-update) | async-done | bytes 1572880 | tf_op jit(solution)/shard_map/all_gather | solution.py:47
  130.8 2.7 reshape.71
  133.5 0.6 fusion.7
  134.1 0.6 copy-done.2
  134.7 0.6 fusion.10
  135.2 102.1 %all-gather.5.cloned.1.call-done = bf16[64,4,3072]{2,1,0:T(4,128)(2,1)} async-done(((bf16[1,4,3072]{2,1,0:T(4,128)(2,1)}), bf16[64,4,3072]{2,1,0:T(4,128)(2,1)}) %all-gather.5.cloned.1.call-update) | async-done | bytes 1572880 | tf_op jit(solution)/shard_map/all_gather | solution.py:48
  237.3 3.7 reshape.69
  241.0 2.2 multiply_convert_fusion.1
  243.2 1.5 fusion.1
  244.7 0.6 fusion.5
  245.3 2.3 convolution_add_fusion
  247.5 448.0 %all-reduce.2 = bf16[256,3072]{1,0:T(8,128)(2,1)} all-reduce(f32[256,3072]{1,0:T(8,128)} %convolution_add_fusion), channel_id=2, replica_groups=mesh['expert'=8,'dp'=64] {'dp'}, use_global_device_ids=true, to_apply=%region_2.3.clone | all-reduce | flops 786432 | bytes 4718592
  695.5 1.0 convolution_convert_fusion.3
  696.6 0.7 reshape.66
  697.3 60.9 %all-to-all-start.2 = ((bf16[8,2,3072]{2,1,0:T(2,128)(2,1)}), bf16[8,2,3072]{2,1,0:T(2,128)(2,1)S(1)}, u32[]{:S(2)}, u32[]{:S(2)}) async-start(bf16[8,2,3072]{2,1,0:T(2,128)(2,1)} %reshape.66), calls=%async_computation.2 | async-start | bytes 196608 | tf_op jit(solution)/shard_map/all_to_all | solution.py:72
  758.1 1.5 fusion
  759.6 1.3 fusion.2
  761.0 2.6 all-to-all-done.2
  763.6 0.6 copy.17
  (11 shorter events, 0.1 us)
Async XLA Ops:
  7.2 126.4 %copy-start = (bf16[1,3072,128]{2,1,0:T(8,128)(2,1)S(1)}, bf16[1,3072,128]{2,1,0:T(8,128)(2,1)}, u32[]{:S(2)}) copy-start(bf16[1,3072,128]{2,1,0:T(8,128)(2,1)} %param.11) | copy-start | bytes 2359300
  7.2 15.8 %all-to-all-start.1 = ((bf16[8,2,3072]{2,1,0:T(2,128)(2,1)}), bf16[8,2,3072]{2,1,0:T(2,128)(2,1)S(1)}, u32[]{:S(2)}, u32[]{:S(2)}) async-start(bf16[8,2,3072]{2,1,0:T(2,128)(2,1)} %bitcast.47), calls=%async_computation.1 | async-start | bytes 196608 | tf_op jit(solution)/shard_map/all_to_all | solution.py:43
  17.5 113.3 %all-gather.7.cloned.1.call-start = ((), (), s32[]{:S(2)}) async-start(), calls=%async_computation.4 | async-start | bytes 1597440 | tf_op jit(solution)/shard_map/all_gather | solution.py:47
  23.8 213.5 %all-gather.5.cloned.1.call-start = ((), (), s32[]{:S(2)}) async-start(), calls=%async_computation.3 | async-start | bytes 1597440 | tf_op jit(solution)/shard_map/all_gather | solution.py:48
  133.5 1.1 copy-start.2
  697.3 66.3 %all-to-all-start.2 = ((bf16[8,2,3072]{2,1,0:T(2,128)(2,1)}), bf16[8,2,3072]{2,1,0:T(2,128)(2,1)S(1)}, u32[]{:S(2)}, u32[]{:S(2)}) async-start(bf16[8,2,3072]{2,1,0:T(2,128)(2,1)} %reshape.66), calls=%async_computation.2 | async-start | bytes 196608 | tf_op jit(solution)/shard_map/all_to_all | solution.py:72
  758.1 1.5 copy-start.1
Sparse Core Ops, SparseCore 0:
  23.9 106.8 all-gather.6
  135.4 101.8 all-gather.4
where the time goes:
time: 772 us; the launch traced here: 771 us
  blocking collectives  458 us (59%)
  waiting for transfers between devices  202 us (26%)
  starting transfers between devices  71.2 us (9%)
  between operations  16.1 us (2%)
  matrix products  13 us (2%)
  local copies, waits for them, and re-layouts  9.87 us (1%)
    unnamed x1, blocking collectives  448 us
    all_gather x1, waiting for transfers between devices, body(): lax.all_gather(pack_rows(got_cots), 'dp', axis=0, tiled=True)  102 us
    all_gather x1, waiting for transfers between devices, body(): lax.all_gather(pack_rows(got_rows), 'dp', axis=0, tiled=True)  93.3 us
    all_to_all x1, starting transfers between devices, body(): lax.all_to_all(slot_grads, 'expert', split_axis=0, concat_axis=0, tiled=T...  60.9 us
  transfers between devices with their start and end apart: 4, of which 4 were waited for; matrix products, arithmetic and copies ran while one was open for 1% of the time, Pallas kernels for 0%

commit v1 on v0

--- a/solution.py
+++ b/solution.py
@@ -44,7 +44,10 @@
         lax.all_to_all(slot_cots, "expert", split_axis=0, concat_axis=0, tiled=True),
     )
     group_rows, group_cots = (
-        lax.all_gather(pack_rows(got_rows), "dp", axis=0, tiled=True),
+        jnp.concatenate(
+            lax.all_to_all(jnp.stack([pack_rows(got_rows)] * lax.axis_size("dp")), "dp", 0, 0),
+            axis=0,
+        ),
         lax.all_gather(pack_rows(got_cots), "dp", axis=0, tiled=True),
     )
     gate_weight = w_gate[0]

time: 772 us -> 740 us (0.959)
  waiting for transfers between devices: 202 us -> 160 us
  starting transfers between devices: 71.2 us -> 87.7 us
    all_gather x1 -> x0, waiting for transfers between devices: 93.3 us -> none  [body(): lax.all_gather(pack_rows(got_rows), 'dp', axis=0, tiled=True)]
    all_gather x1, waiting for transfers between devices: 102 us -> 148 us  [body(): lax.all_gather(pack_rows(got_cots), 'dp', axis=0, tiled=True)]
    all_to_all x0 -> x2, starting transfers between devices: none -> 19.9 us  [the longest x1 15.8 us: body(): lax.all_to_all(jnp.stack([pack_rows(got_rows)] * lax.axis_size('dp')), 'd...]
    all_to_all x1 -> x0, blocking collectives: 9.62 us -> none  [body(): lax.all_to_all(slot_cots, 'expert', split_axis=0, concat_axis=0, tiled=True)]
  transfers between devices with their start and end apart: 4 -> 5, of which waited for: 4 -> 4; matrix products, arithmetic and copies ran while one was open for 1% -> 1% of each run, Pallas kernels for 0% -> 0%
where the time goes in v1:
time: 740 us; the launch traced here: 739 us
  blocking collectives  451 us (61%)
  waiting for transfers between devices  160 us (22%)
  starting transfers between devices  87.7 us (12%)
  between operations  16.1 us (2%)
  local copies, waits for them, and re-layouts  12.5 us (2%)
  matrix products  10.7 us (1%)
    unnamed x1, blocking collectives  451 us
    all_gather x1, waiting for transfers between devices, body(): lax.all_gather(pack_rows(got_cots), 'dp', axis=0, tiled=True)  148 us
    all_to_all x1, starting transfers between devices, body(): lax.all_to_all(slot_grads, 'expert', split_axis=0, concat_axis=0, tiled=T...  57.4 us
    all_to_all x1, starting transfers between devices, body(): lax.all_to_all(jnp.stack([pack_rows(got_rows)] * lax.axis_size('dp')), 'd...  15.8 us
  transfers between devices with their start and end apart: 5, of which 4 were waited for; matrix products, arithmetic and copies ran while one was open for 1% of the time, Pallas kernels for 0%

profile of v1, /device:TPU:1, one launch (start us, length us, event | category | flops | bytes accessed | tf_op | source)
XLA Modules:
  0.0 739.1 jit_solution(2863188146307534223)
XLA Ops:
  7.2 10.3 %all-to-all-start.1 = ((bf16[8,2,3072]{2,1,0:T(2,128)(2,1)}), bf16[8,2,3072]{2,1,0:T(2,128)(2,1)S(1)}, u32[]{:S(2)}, u32[]{:S(2)}) async-start(bf16[8,2,3072]{2,1,0:T(2,128)(2,1)} %bitcast.45), calls=%async_computation.1 | async-start | bytes 196608 | tf_op jit(solution)/shard_map/all_to_all | solution.py:43
  17.5 0.8 select_reduce_fusion.1
  18.3 0.1 lt.30
  18.4 0.1 select_reduce_fusion
  18.6 4.4 all-to-all-done.1
  23.0 4.1 all-to-all-start
  27.3 0.1 convolution_convert_fusion.4
  27.4 5.2 all-to-all-done
  32.6 1.6 stack.2
  34.2 15.8 %all-to-all-start.2 = ((bf16[64,4,3072]{2,1,0:T(4,128)(2,1)}), bf16[64,4,3072]{2,1,0:T(4,128)(2,1)}, u32[]{:S(2)}, u32[]{:S(2)}) async-start(bf16[64,4,3072]{2,1,0:T(4,128)(2,1)} %stack.2), calls=%async_computation.2 | async-start | bytes 3145728 | tf_op jit(solution)/shard_map/all_to_all | solution.py:48
  50.0 0.7 fusion.3
  52.1 1.3 dynamic-slice
  54.0 147.9 %all-gather.3.cloned.1.call-done = bf16[64,4,3072]{2,1,0:T(4,128)(2,1)} async-done(((bf16[1,4,3072]{2,1,0:T(4,128)(2,1)}), bf16[64,4,3072]{2,1,0:T(4,128)(2,1)}) %all-gather.3.cloned.1.call-update) | async-done | bytes 1572880 | tf_op jit(solution)/shard_map/all_gather | solution.py:51
  202.0 3.7 reshape.75
  205.7 2.7 reshape.69
  208.4 0.6 fusion.6
  209.0 0.6 copy-done.3
  209.6 0.6 fusion.9
  210.2 0.8 copy-done.1
  211.0 0.2 copy-done.4
  211.2 0.6 multiply_convert_fusion.1
  211.8 1.5 fusion.1
  213.3 0.6 fusion.4
  213.8 2.2 convolution_add_fusion
  216.1 450.9 %all-reduce.2 = bf16[256,3072]{1,0:T(8,128)(2,1)} all-reduce(f32[256,3072]{1,0:T(8,128)} %convolution_add_fusion), channel_id=2, replica_groups=mesh['expert'=8,'dp'=64] {'dp'}, use_global_device_ids=true, to_apply=%region_2.3.clone | all-reduce | flops 786432 | bytes 4718592
  667.0 1.0 convolution_convert_fusion.3
  668.0 0.7 reshape.72
  668.7 57.4 %all-to-all-start.3 = ((bf16[8,2,3072]{2,1,0:T(2,128)(2,1)}), bf16[8,2,3072]{2,1,0:T(2,128)(2,1)S(1)}, u32[]{:S(2)}, u32[]{:S(2)}) async-start(bf16[8,2,3072]{2,1,0:T(2,128)(2,1)} %reshape.72), calls=%async_computation.3 | async-start | bytes 196608 | tf_op jit(solution)/shard_map/all_to_all | solution.py:75
  726.1 1.5 fusion
  727.6 1.3 fusion.2
  729.0 2.6 all-to-all-done.3
  731.6 0.6 copy.17
  (16 shorter events, 0.4 us)
Async XLA Ops:
  7.2 201.3 %copy-start = (bf16[1,3072,128]{2,1,0:T(8,128)(2,1)S(1)}, bf16[1,3072,128]{2,1,0:T(8,128)(2,1)}, u32[]{:S(2)}) copy-start(bf16[1,3072,128]{2,1,0:T(8,128)(2,1)} %param.11) | copy-start | bytes 2359300
  7.2 15.8 %all-to-all-start.1 = ((bf16[8,2,3072]{2,1,0:T(2,128)(2,1)}), bf16[8,2,3072]{2,1,0:T(2,128)(2,1)S(1)}, u32[]{:S(2)}, u32[]{:S(2)}) async-start(bf16[8,2,3072]{2,1,0:T(2,128)(2,1)} %bitcast.45), calls=%async_computation.1 | async-start | bytes 196608 | tf_op jit(solution)/shard_map/all_to_all | solution.py:43
  23.0 9.6 %all-to-all-start = ((bf16[8,2,3072]{2,1,0:T(2,128)(2,1)}), bf16[8,2,3072]{2,1,0:T(2,128)(2,1)S(1)}, u32[]{:S(2)}, u32[]{:S(2)}) async-start(bf16[8,2,3072]{2,1,0:T(2,128)(2,1)} %bitcast.46), calls=%async_computation | async-start | bytes 196608 | tf_op jit(solution)/shard_map/all_to_all | solution.py:44
  34.2 171.5 %all-to-all-start.2 = ((bf16[64,4,3072]{2,1,0:T(4,128)(2,1)}), bf16[64,4,3072]{2,1,0:T(4,128)(2,1)}, u32[]{:S(2)}, u32[]{:S(2)}) async-start(bf16[64,4,3072]{2,1,0:T(4,128)(2,1)} %stack.2), calls=%async_computation.2 | async-start | bytes 3145728 | tf_op jit(solution)/shard_map/all_to_all | solution.py:48
  49.9 152.0 %all-gather.3.cloned.1.call-start = ((), (), s32[]{:S(2)}) async-start(), calls=%async_computation.4 | async-start | bytes 1597440 | tf_op jit(solution)/shard_map/all_gather | solution.py:51
  208.4 1.1 copy-start.3
  209.6 1.4 copy-start.1
  209.6 1.6 copy-start.4
  668.7 62.9 %all-to-all-start.3 = ((bf16[8,2,3072]{2,1,0:T(2,128)(2,1)}), bf16[8,2,3072]{2,1,0:T(2,128)(2,1)S(1)}, u32[]{:S(2)}, u32[]{:S(2)}) async-start(bf16[8,2,3072]{2,1,0:T(2,128)(2,1)} %reshape.72), calls=%async_computation.3 | async-start | bytes 196608 | tf_op jit(solution)/shard_map/all_to_all | solution.py:75
  726.1 1.5 copy-start.2
Sparse Core Ops, SparseCore 0:
  55.4 146.4 all-gather.2
